TPU v7x, 32 devices: a whole 2x2x4 slice. The times are simulated.
32 devices in a mesh: row: 8 (over y, x, core), col: 4 (over z).
Axes of the slice: x: 2, y: 2, z: 4, core: 2. Of those that a mesh axis runs over, the one named last changes fastest.
Arguments:
- owned_rows: bfloat16 [768, 8192], P(('row', 'col')), may hold values from -6 to 6
- suffix_lengths: int32 [32], replicated, may hold values from 1 to 24, 256 in all
- owner_map: int32 [32], replicated, may hold values from 0 to 31, each once
- prefix_lengths: int32 [32], replicated, may hold values from 0 to 4095
- gate_weight: bfloat16 [8192, 29568], P('row', 'col'), may hold values from -0.0625 to 0.0625
- up_weight: bfloat16 [8192, 29568], P('row', 'col'), may hold values from -0.0625 to 0.0625
- down_weight: bfloat16 [29568, 8192], P('col', 'row'), may hold values from -0.03125 to 0.03125
Outputs:
- mixed: bfloat16 [256, 8192], P('col', 'row')
Inputs may be any that keep to these rules, and one draw needn't show every extreme that they name: `suffix_lengths`: the lengths add up to 256; the largest is exactly 24. `owner_map`: each device owns one request; request r's suffix rows fill, in order, the first suffix_lengths[r] of the 24 slots of its owner in owned_rows, and the other slots are not used.
All inputs are finite; a program needn't handle non-finite values.
Results may differ from a plain program's by a relative error of at most 0.0049.
Values may be sent and summed in bfloat16 or wider, within the bound.
A program may use at most 128 MiB of HBM per device.

v0:
```python
import jax
import jax.numpy as jnp
from jax import lax
from jax.sharding import PartitionSpec as P

TOK_DEV = 8


def source_rows(suffix_lengths, owner_map, prefix_lengths, row_count, slot_size):
    request_ids = jnp.arange(suffix_lengths.shape[0], dtype=jnp.int32)
    longer = prefix_lengths[None, :] > prefix_lengths[:, None]
    earlier = (prefix_lengths[None, :] == prefix_lengths[:, None]) & (
        request_ids[None, :] < request_ids[:, None]
    )
    starts = jnp.sum(jnp.where(longer | earlier, suffix_lengths[None, :], 0), axis=1)
    positions = jnp.arange(row_count, dtype=jnp.int32)
    ends = starts + suffix_lengths
    inside = (positions[:, None] >= starts[None, :]) & (positions[:, None] < ends[None, :])
    offsets = owner_map * slot_size - starts
    shifted = jnp.sum(jnp.where(inside, offsets[None, :], 0), axis=1)
    return positions + shifted


def on_device(
    owned_rows, suffix_lengths, owner_map, prefix_lengths, gate_weight, up_weight, down_weight
):
    row_count = lax.axis_size("row")
    col_count = lax.axis_size("col")
    slot_size = owned_rows.shape[0]
    total_rows = TOK_DEV * suffix_lengths.shape[0]
    feature_width = owned_rows.shape[1] // row_count
    source = source_rows(suffix_lengths, owner_map, prefix_lengths, total_rows, slot_size)
    feature_rows = lax.all_to_all(owned_rows, "row", split_axis=1, concat_axis=0, tiled=True)
    owner_index = source // slot_size
    within = source % slot_size
    gathered_index = (
        owner_index % col_count * row_count + owner_index // col_count
    ) * slot_size + within
    piece = lax.all_gather(feature_rows, "col", axis=0, tiled=True)
    keep_mask = (gathered_index >= 0) & (gathered_index < piece.shape[0])
    picked = jnp.take(piece, jnp.clip(gathered_index, 0, piece.shape[0] - 1), axis=0)
    suffix_rows = jnp.where(
        keep_mask[:, None], picked, jnp.zeros((total_rows, feature_width), jnp.bfloat16)
    )
    block_rows = suffix_rows
    gate_share = lax.psum_scatter(
        jnp.dot(block_rows, gate_weight, preferred_element_type=jnp.float32),
        "row",
        scatter_dimension=0,
        tiled=True,
    )
    block_rows = suffix_rows
    up_share = lax.psum_scatter(
        jnp.dot(block_rows, up_weight, preferred_element_type=jnp.float32),
        "row",
        scatter_dimension=0,
        tiled=True,
    )
    hidden_share = (jax.nn.silu(gate_share) * up_share).astype(jnp.bfloat16)
    partial_sums = jnp.dot(
        lax.all_gather(hidden_share, "row", axis=0, tiled=True),
        down_weight,
        preferred_element_type=jnp.float32,
    )
    return lax.psum_scatter(partial_sums, "col", scatter_dimension=0, tiled=True).astype(
        jnp.bfloat16
    )


def solution(mesh):
    return jax.shard_map(
        on_device,
        mesh=mesh,
        in_specs=(
            P(("row", "col"), None),
            P(),
            P(),
            P(),
            P("row", "col"),
            P("row", "col"),
            P("col", "row"),
        ),
        out_specs=P("col", "row"),
        check_vma=False,
    )
```

profile of v0, /device:TPU:0, one launch (start us, length us, event | category | flops | bytes accessed | tf_op | source)
XLA Modules:
  0.0 302.0 jit_solution(13955425975562935703)
XLA Ops:
  6.5 0.0 all-gather.3.cloned.1.call-start
  6.5 1.0 copy.13
  7.6 13.4 %all_to_all.19 = bf16[24,8,1024]{2,0,1:T(8,128)(2,1)} all-to-all(bf16[24,8,1024]{2,0,1:T(8,128)(2,1)S(1)} %bitcast.14), channel_id=1, replica_groups=mesh['row'=8,'col'=4] {'row'}, dimensions={1} | all-to-all | bytes 786432 | tf_op jit(solution)/shard_map/all_to_all | solution.py:33
  21.0 0.0 all-gather.3.cloned.1.call-update
  21.0 0.0 reduce-scatter.6.cloned.1.call-start
  21.1 0.9 select_reduce_fusion.1
  22.0 0.7 fusion.12
  22.6 0.1 select_reduce_fusion
  22.8 34.8 %all-gather.3.cloned.1.call-done = bf16[768,1024]{1,0:T(8,128)(2,1)} async-done(((bf16[192,1024]{1,0:T(8,128)(2,1)}), bf16[768,1024]{1,0:T(8,128)(2,1)}) %all-gather.3.cloned.1.call-update) | async-done | bytes 1572880 | tf_op jit(solution)/shard_map/all_gather | solution.py:39
  57.6 3.2 %gather_fusion = bf16[256,1024]{1,0:T(8,128)(2,1)S(1)} fusion(bf16[768,1024]{1,0:T(8,128)(2,1)} %all-gather.3.cloned.1.call-done, s32[1024]{0:T(1024)S(1)} %pad_clamp_fusion), kind=kCustom, calls=%fused_computation | custom fusion | bytes 1049600 | tf_op jit(solution)/shard_map/jit(_take)/gather | solution.py:41
  60.8 17.2 %fusion.9 = f32[256,7392]{1,0:T(8,128)} fusion(bf16[1024,7392]{0,1:T(8,128)(2,1)} %param.12, bf16[256,1024]{1,0:T(8,128)(2,1)S(1)} %gather_fusion, pred[256]{0:T(512)(128)(4,1)S(1)} %compare_and_fusion, pred[256]{0:T(512)(128)(4,1)S(1)} %get-tuple-element.5), kind=kOutput, calls=%fused_computation.38 | convolution fusion | flops 3876061184 | bytes 23233024 | tf_op jit(solution)/shard_map/dot_general | solution.py:54
  78.0 0.0 reduce-scatter.6.cloned.1.call-update
  78.0 0.0 reduce-scatter.4.cloned.1.call-start
  78.1 17.9 %fusion.10 = f32[256,7392]{1,0:T(8,128)} fusion(bf16[1024,7392]{0,1:T(8,128)(2,1)} %param.11, bf16[256,1024]{1,0:T(8,128)(2,1)S(1)} %gather_fusion, pred[256]{0:T(512)(128)(4,1)S(1)} %compare_and_fusion, pred[256]{0:T(512)(128)(4,1)S(1)} %get-tuple-element.5), kind=kOutput, calls=%fused_computation.39 | convolution fusion | flops 3876061184 | bytes 23233024 | tf_op jit(solution)/shard_map/dot_general | solution.py:47
  96.0 0.0 reduce-scatter.4.cloned.1.call-update
  96.0 0.0 all-gather.5.cloned.1.call-start
  96.1 49.2 %reduce-scatter.6.cloned.1.call-done = f32[32,7392]{1,0:T(8,128)} async-done(((f32[256,7392]{1,0:T(8,128)}), f32[32,7392]{1,0:T(8,128)}) %reduce-scatter.6.cloned.1.call-update) | async-done | bytes 946192 | tf_op jit(solution)/shard_map/reduce_scatter | solution.py:53
  145.2 72.0 %reduce-scatter.4.cloned.1.call-done = f32[32,7392]{1,0:T(8,128)} async-done(((f32[256,7392]{1,0:T(8,128)}), f32[32,7392]{1,0:T(8,128)}) %reduce-scatter.4.cloned.1.call-update) | async-done | bytes 946192 | tf_op jit(solution)/shard_map/reduce_scatter | solution.py:46
  217.3 2.5 multiply_convert_fusion
  219.8 0.0 all-gather.5.cloned.1.call-update
  219.8 0.2 reduce-scatter.8.cloned.1.call-start
  220.0 35.0 %all-gather.5.cloned.1.call-done = bf16[256,7392]{1,0:T(8,128)(2,1)} async-done(((bf16[32,7392]{1,0:T(8,128)(2,1)}), bf16[256,7392]{1,0:T(8,128)(2,1)}) %all-gather.5.cloned.1.call-update) | async-done | bytes 3784720 | tf_op jit(solution)/shard_map/all_gather | solution.py:61
  255.0 11.5 %fusion.13 = f32[256,1024]{1,0:T(8,128)} fusion(bf16[256,7392]{1,0:T(8,128)(2,1)} %all-gather.5.cloned.1.call-done, bf16[7392,1024]{1,0:T(8,128)(2,1)} %param.13), kind=kOutput, calls=%fused_computation.41 | convolution fusion | flops 3875536896 | bytes 19972096 | tf_op jit(solution)/shard_map/dot_general | solution.py:60
  266.5 0.0 reduce-scatter.8.cloned.1.call-update
  266.6 27.3 %reduce-scatter.8.cloned.1.call-done = f32[64,1024]{1,0:T(8,128)} async-done(((f32[256,1024]{1,0:T(8,128)}), f32[64,1024]{1,0:T(8,128)}) %reduce-scatter.8.cloned.1.call-update) | async-done | bytes 262160 | tf_op jit(solution)/shard_map/reduce_scatter | solution.py:65
  293.9 1.6 convert_element_type.7
  (4 shorter events, 0.1 us)
Async XLA Ops:
  6.5 51.1 %all-gather.3.cloned.1.call-start = ((), (), s32[]{:S(2)}) async-start(), calls=%async_computation.4 | async-start | bytes 1966080 | tf_op jit(solution)/shard_map/all_gather | solution.py:39
  21.0 124.2 %reduce-scatter.6.cloned.1.call-start = ((), (), s32[]{:S(2)}) async-start(), calls=%async_computation.6 | async-start | bytes 8552448 | tf_op jit(solution)/shard_map/reduce_scatter | solution.py:53
  78.0 139.2 %reduce-scatter.4.cloned.1.call-start = ((), (), s32[]{:S(2)}) async-start(), calls=%async_computation.5 | async-start | bytes 8552448 | tf_op jit(solution)/shard_map/reduce_scatter | solution.py:46
  96.0 159.0 %all-gather.5.cloned.1.call-start = ((), (), s32[]{:S(2)}) async-start(), calls=%async_computation.7 | async-start | bytes 4276224 | tf_op jit(solution)/shard_map/all_gather | solution.py:61
  219.8 74.1 %reduce-scatter.8.cloned.1.call-start = ((), (), s32[]{:S(2)}) async-start(), calls=%async_computation.8 | async-start | bytes 1310720 | tf_op jit(solution)/shard_map/reduce_scatter | solution.py:65
Sparse Core Ops, SparseCore 0:
  21.1 36.4 all-gather.2
  78.2 67.0 reduce-scatter.5
  149.1 68.1 reduce-scatter.3
  219.9 35.0 all-gather.4
  266.7 27.1 reduce-scatter.7
where the time goes:
time: 302 us
  waiting for transfers between devices  218 us (72%)
  matrix products  46.6 us (15%)
  blocking collectives  13.4 us (4%)
  between operations  13.2 us (4%)
  other arithmetic  5.89 us (2%)
  local copies, waits for them, and re-layouts  4.19 us (1%)
    reduce_scatter x1, waiting for transfers between devices, on_device(): lax.psum_scatter(jnp.dot(block_rows, gate_weight, preferred_element_type=...  72 us
    reduce_scatter x1, waiting for transfers between devices, on_device(): lax.psum_scatter(jnp.dot(block_rows, up_weight, preferred_element_type=jn...  49.2 us
    all_gather x1, waiting for transfers between devices, on_device(): lax.all_gather(hidden_share, 'row', axis=0, tiled=True)  35 us
    all_gather x1, waiting for transfers between devices, on_device(): piece = lax.all_gather(feature_rows, 'col', axis=0, tiled=True)  34.8 us
    reduce_scatter x1, waiting for transfers between devices, on_device(): lax.psum_scatter(partial_sums, 'col', scatter_dimension=0, tiled=True)  27.3 us
    dot_general x1, matrix products, on_device(): jnp.dot(block_rows, gate_weight, preferred_element_type=jnp.float32)  17.9 us
    dot_general x1, matrix products, on_device(): jnp.dot(block_rows, up_weight, preferred_element_type=jnp.float32)  17.2 us
    all_to_all x1, blocking collectives, on_device(): lax.all_to_all(owned_rows, 'row', split_axis=1, concat_axis=0, tiled=True)  13.4 us
  transfers between devices with their start and end apart: 5, of which 5 were waited for; matrix products, arithmetic and copies ran while one was open for 7% of the time, Pallas kernels for 0%

commit v1 on v0

v1 whole, which is shorter than its diff:
```python
import functools

import jax
import jax.numpy as jnp
from jax import lax
from jax.experimental import pallas as pl
from jax.experimental.pallas import tpu as pltpu
from jax.sharding import PartitionSpec as P

TOK_DEV = 8
CHUNK = 512
LAG = 1
WEIGHT_SLOTS = 4
MESH = pl.DeviceIdType.MESH


def source_rows(suffix_lengths, owner_map, prefix_lengths, row_count, slot_size):
    request_ids = jnp.arange(suffix_lengths.shape[0], dtype=jnp.int32)
    longer = prefix_lengths[None, :] > prefix_lengths[:, None]
    earlier = (prefix_lengths[None, :] == prefix_lengths[:, None]) & (
        request_ids[None, :] < request_ids[:, None]
    )
    starts = jnp.sum(jnp.where(longer | earlier, suffix_lengths[None, :], 0), axis=1)
    positions = jnp.arange(row_count, dtype=jnp.int32)
    ends = starts + suffix_lengths
    inside = (positions[:, None] >= starts[None, :]) & (positions[:, None] < ends[None, :])
    offsets = owner_map * slot_size - starts
    shifted = jnp.sum(jnp.where(inside, offsets[None, :], 0), axis=1)
    return positions + shifted


def layer_kernel(
    n, cols, chunks,
    x_ref, gate_ref, up_ref, down_ref, gate_tail, up_tail, down_tail,
    out_ref, *scratch,
):
    k = n.bit_length() - 1
    tokens, width = x_ref.shape[0], gate_tail.shape[1]
    half = tokens // 2
    block = half >> k
    out_width = down_ref.shape[1]
    slots, hidden_slots = 2 * LAG, (k + 1) * LAG
    parts = list(scratch)
    product, hidden, total, gate_w, up_w, down_w, col_out, col_in = parts[:8]
    received = parts[8 : 8 + k]
    outgoing = [None] + parts[8 + k : 7 + 2 * k]
    kept = [None] + parts[7 + 2 * k : 6 + 3 * k]
    send_sem, recv_sem, gather_send, gather_recv, weight_sem, col_send, col_recv = parts[6 + 3 * k :]

    me = lax.axis_index("row")
    my_col = lax.axis_index("col")
    bits = [(me // (1 << b)) % 2 for b in range(k)]
    partners = [me + (1 - 2 * bits[b]) * (1 << b) for b in range(k)]
    orders = [list(range(k)), [0] + list(range(k - 1, 0, -1))]
    places = [sum(bits[b] * (1 << (k - 1 - i)) for i, b in enumerate(order)) for order in orders]

    barrier = pltpu.get_barrier_semaphore()
    for partner in partners:
        pl.semaphore_signal(barrier, inc=1, device_id=(partner, my_col), device_id_type=MESH)
    for step in range(1, cols):
        other = (my_col + step) % cols
        pl.semaphore_signal(barrier, inc=1, device_id=(me, other), device_id_type=MESH)
    pl.semaphore_wait(barrier, k + cols - 1)

    def load(array, tail, buffer, kind, j, by_rows):
        slot = j % WEIGHT_SLOTS
        sem = weight_sem.at[kind, slot]

        @pl.when(j < chunks - 1)
        def _():
            at = pl.ds(pl.multiple_of(j * width, width), width)
            piece = array.at[at, :] if by_rows else array.at[:, at]
            pltpu.make_async_copy(piece, buffer.at[slot], sem).start()

        @pl.when(j == chunks - 1)
        def _():
            pltpu.make_async_copy(tail, buffer.at[slot], sem).start()

    def loaded(tail, buffer, kind, j):
        slot = j % WEIGHT_SLOTS
        pltpu.make_async_copy(tail, buffer.at[slot], weight_sem.at[kind, slot]).wait()

    def load_in(j):
        load(gate_ref, gate_tail, gate_w, 0, j, False)
        load(up_ref, up_tail, up_w, 1, j, False)

    def load_down(j):
        load(down_ref, down_tail, down_w, 2, j, True)

    def exchange(s, h, j):
        slot = j % slots
        b = orders[h][s]
        size = half >> (s + 1)
        if s == 0:
            source = product.at[slot, pl.ds(pl.multiple_of(h * half + (1 - bits[b]) * size, size), size), :]
        else:
            source = outgoing[s].at[slot, h]
        return pltpu.make_async_remote_copy(
            src_ref=source,
            dst_ref=received[s].at[slot, h],
            send_sem=send_sem.at[s, h, slot],
            recv_sem=recv_sem.at[s, h, slot],
            device_id=(partners[b], my_col),
            device_id_type=MESH,
        )

    def gather(i, h, j):
        slot = j % hidden_slots
        b = orders[h][k - 1 - i]
        size = block << i
        at = pl.ds(pl.multiple_of(h * half + places[h] // (1 << i) * size, size), size)
        return pltpu.make_async_remote_copy(
            src_ref=hidden.at[slot, at, :],
            dst_ref=hidden.at[slot, at, :],
            send_sem=gather_send.at[i, h, slot],
            recv_sem=gather_recv.at[i, h, slot],
            device_id=(partners[b], my_col),
            device_id_type=MESH,
        )

    def rows_of(s, h, j, first, size):
        slot = j % slots
        if s == 1:
            at = pl.multiple_of(h * half + bits[orders[h][0]] * (half >> 1) + first, size)
            own = product[slot, pl.ds(at, size), :]
        else:
            own = kept[s - 1][slot, h, pl.ds(first, size), :]
        return own + received[s - 1][slot, h, pl.ds(first, size), :].astype(jnp.float32)

    def halve(s, j):
        size = half >> (s + 1)
        for h in range(2):
            exchange(s - 1, h, j).wait()
            bit = bits[orders[h][s]]
            away = pl.multiple_of((1 - bit) * size, size)
            outgoing[s][j % slots, h] = rows_of(s, h, j, away, size).astype(jnp.bfloat16)
            exchange(s, h, j).start()
        for h in range(2):
            bit = bits[orders[h][s]]
            stay = pl.multiple_of(bit * size, size)
            kept[s][j % slots, h] = rows_of(s, h, j, stay, size)

    def activate(j):
        for h in range(2):
            exchange(k - 1, h, j).wait()
            sums = rows_of(k, h, j, 0, block)
            gate, up = sums[:, :width], sums[:, width:]
            at = pl.multiple_of(h * half + places[h] * block, block)
            value = (gate / (1.0 + jnp.exp(-gate)) * up).astype(jnp.bfloat16)
            hidden[j % hidden_slots, pl.ds(at, block), :] = value
            gather(0, h, j).start()

    def spread(i, j):
        for h in range(2):
            gather(i - 1, h, j).wait_recv()
            gather(i, h, j).start()

    def down(j):
        for h in range(2):
            gather(k - 1, h, j).wait_recv()
        loaded(down_tail, down_w, 2, j)
        total[...] += jnp.dot(
            hidden[j % hidden_slots], down_w[j % WEIGHT_SLOTS], preferred_element_type=jnp.float32
        )
        for i in range(k):
            for h in range(2):
                gather(i, h, j).wait_send()

    def project(j):
        slot = j % slots
        loaded(gate_tail, gate_w, 0, j)
        loaded(up_tail, up_w, 1, j)
        x = x_ref[...]
        product[slot, :, :width] = jnp.dot(
            x, gate_w[j % WEIGHT_SLOTS], preferred_element_type=jnp.float32
        )
        product[slot, :, width:] = jnp.dot(
            x, up_w[j % WEIGHT_SLOTS], preferred_element_type=jnp.float32
        )
        for h in range(2):
            exchange(0, h, j).start()

    steps = [project]
    steps += [functools.partial(halve, s) for s in range(1, k)]
    steps += [activate]
    steps += [functools.partial(spread, i) for i in range(1, k)]
    steps += [down]

    ahead = WEIGHT_SLOTS - 1
    for j in range(min(ahead, chunks)):
        load_in(jnp.int32(j))
        load_down(jnp.int32(j))
    total[...] = jnp.zeros_like(total)
    last = len(steps) - 1

    def round_of(t, carry):
        @pl.when(t + ahead < chunks)
        def _():
            load_in(t + ahead)

        j_down = t - last * LAG + ahead

        @pl.when((j_down >= ahead) & (j_down < chunks))
        def _():
            load_down(j_down)

        for s in range(last, -1, -1):
            j = t - s * LAG

            @pl.when((j >= 0) & (j < chunks))
            def _():
                steps[s](j)

        return carry

    lax.fori_loop(0, chunks + last * LAG, round_of, 0)

    share = tokens // cols
    copies = []
    for step in range(1, cols):
        other = (my_col + step) % cols
        rows = total[pl.ds(pl.multiple_of(other * share, share), share), :]
        col_out[step - 1] = rows.astype(jnp.bfloat16)
        copy = pltpu.make_async_remote_copy(
            src_ref=col_out.at[step - 1],
            dst_ref=col_in.at[step - 1],
            send_sem=col_send.at[step - 1],
            recv_sem=col_recv.at[step - 1],
            device_id=(me, other),
            device_id_type=MESH,
        )
        copy.start()
        copies.append(copy)
    result = total[pl.ds(pl.multiple_of(my_col * share, share), share), :]
    for step, copy in enumerate(copies):
        copy.wait()
        result = result + col_in[step].astype(jnp.float32)
    out_ref[...] = result.astype(jnp.bfloat16)


def layer(x, gate_weight, up_weight, down_weight, n, cols):
    tokens, depth = x.shape
    units = gate_weight.shape[1]
    out_width = down_weight.shape[1]
    width = CHUNK
    chunks = -(-units // width)
    start = (chunks - 1) * width
    short = width - (units - start)
    gate_tail = jnp.pad(gate_weight[:, start:], ((0, 0), (0, short)))
    up_tail = jnp.pad(up_weight[:, start:], ((0, 0), (0, short)))
    down_tail = jnp.pad(down_weight[start:], ((0, short), (0, 0)))
    k = n.bit_length() - 1
    half = tokens // 2
    slots, hidden_slots = 2 * LAG, (k + 1) * LAG
    share = tokens // cols
    bf16, f32 = jnp.bfloat16, jnp.float32
    sizes = [half >> (s + 1) for s in range(k)]
    scratch = [
        pltpu.VMEM((slots, tokens, 2 * width), f32),
        pltpu.VMEM((hidden_slots, tokens, width), bf16),
        pltpu.VMEM((tokens, out_width), f32),
        pltpu.VMEM((WEIGHT_SLOTS, depth, width), bf16),
        pltpu.VMEM((WEIGHT_SLOTS, depth, width), bf16),
        pltpu.VMEM((WEIGHT_SLOTS, width, out_width), bf16),
        pltpu.VMEM((cols - 1, share, out_width), bf16),
        pltpu.VMEM((cols - 1, share, out_width), bf16),
    ]
    scratch += [
        pltpu.VMEM((slots, 2, size, 2 * width), f32 if s == 0 else bf16)
        for s, size in enumerate(sizes)
    ]
    scratch += [pltpu.VMEM((slots, 2, size, 2 * width), bf16) for size in sizes[1:]]
    scratch += [pltpu.VMEM((slots, 2, size, 2 * width), f32) for size in sizes[1:]]
    dma = pltpu.SemaphoreType.DMA
    scratch += [
        dma((k, 2, slots)),
        dma((k, 2, slots)),
        dma((k, 2, hidden_slots)),
        dma((k, 2, hidden_slots)),
        dma((3, WEIGHT_SLOTS)),
        dma((cols - 1,)),
        dma((cols - 1,)),
    ]
    vmem = pl.BlockSpec(memory_space=pltpu.VMEM)
    hbm = pl.BlockSpec(memory_space=pl.ANY)
    return pl.pallas_call(
        functools.partial(layer_kernel, n, cols, chunks),
        out_shape=jax.ShapeDtypeStruct((share, out_width), bf16),
        in_specs=[vmem] + [hbm] * 6,
        out_specs=vmem,
        scratch_shapes=scratch,
        compiler_params=pltpu.CompilerParams(
            collective_id=0, has_side_effects=True, vmem_limit_bytes=56 * 1024 * 1024
        ),
        cost_estimate=pl.CostEstimate(
            flops=6 * tokens * depth * units,
            bytes_accessed=6 * depth * units,
            transcendentals=tokens * units // n,
        ),
    )(x, gate_weight, up_weight, down_weight, gate_tail, up_tail, down_tail)


def on_device(
    owned_rows, suffix_lengths, owner_map, prefix_lengths, gate_weight, up_weight, down_weight
):
    row_count = lax.axis_size("row")
    col_count = lax.axis_size("col")
    slot_size = owned_rows.shape[0]
    total_rows = TOK_DEV * suffix_lengths.shape[0]
    source = source_rows(suffix_lengths, owner_map, prefix_lengths, total_rows, slot_size)
    feature_rows = lax.all_to_all(owned_rows, "row", split_axis=1, concat_axis=0, tiled=True)
    owner_index = source // slot_size
    within = source % slot_size
    gathered_index = (
        owner_index % col_count * row_count + owner_index // col_count
    ) * slot_size + within
    piece = lax.all_gather(feature_rows, "col", axis=0, tiled=True)
    suffix_rows = jnp.take(piece, gathered_index, axis=0, mode="clip")
    return layer(suffix_rows, gate_weight, up_weight, down_weight, row_count, col_count)


def solution(mesh):
    return jax.shard_map(
        on_device,
        mesh=mesh,
        in_specs=(
            P(("row", "col"), None),
            P(),
            P(),
            P(),
            P("row", "col"),
            P("row", "col"),
            P("col", "row"),
        ),
        out_specs=P("col", "row"),
        check_vma=False,
    )
```

time: 302 us -> 167 us (0.55)
  waiting for transfers between devices: 218 us -> 0.04 us
  Pallas kernels: 0 us -> 89.1 us
  matrix products: 46.6 us -> 0 us
  local copies, waits for them, and re-layouts: 4.19 us -> 49.1 us
  other arithmetic: 5.89 us -> 0.32 us
    reduce_scatter x3 -> x0, waiting for transfers between devices: 149 us -> none  [the longest x1 72 us: on_device(): lax.psum_scatter(jnp.dot(block_rows, gate_weight, preferred_element_type=...]
    pallas_call x0 -> x1, Pallas kernels: none -> 89.1 us  [layer(): pl.pallas_call(functools.partial(layer_kernel, n, cols, chunks), out_shap...]
    dot_general x3 -> x0, matrix products: 46.6 us -> none  [the longest x1 17.9 us: on_device(): jnp.dot(block_rows, gate_weight, preferred_element_type=jnp.float32)]
    unnamed x0 -> x9, local copies, waits for them, and re-layouts: none -> 39.7 us
    all_gather x1 -> x0, waiting for transfers between devices: 35 us -> none  [on_device(): lax.all_gather(hidden_share, 'row', axis=0, tiled=True)]
    all_gather x1, waiting for transfers between devices: 34.8 us -> 0.02 us  [on_device(): piece = lax.all_gather(feature_rows, 'col', axis=0, tiled=True)]
    convert_element_type x2 -> x0, other arithmetic: 4.12 us -> none  [the longest x1 2.5 us: on_device(): hidden_share = (jax.nn.silu(gate_share) * up_share).astype(jnp.bfloat16)]
    pad x0 -> x3, local copies, waits for them, and re-layouts: none -> 3.34 us  [the longest x1 1.13 us: layer(): up_tail = jnp.pad(up_weight[:, start:], ((0, 0), (0, short)))]
  transfers between devices with their start and end apart: 5 -> 1, of which waited for: 5 -> 0; matrix products, arithmetic and copies ran while one was open for 7% -> 26% of each run, Pallas kernels for 0% -> 0%
where the time goes in v1:
time: 167 us; the launch traced here: 165 us
  Pallas kernels  89.1 us (53%)
  local copies, waits for them, and re-layouts  49.1 us (29%)
  between operations  13.5 us (8%)
  blocking collectives  13.4 us (8%)
    pallas_call x1, Pallas kernels, layer(): pl.pallas_call(functools.partial(layer_kernel, n, cols, chunks), out_shap...  89.1 us
    unnamed x9, local copies, waits for them, and re-layouts  39.7 us
    all_to_all x1, blocking collectives, on_device(): lax.all_to_all(owned_rows, 'row', split_axis=1, concat_axis=0, tiled=True)  13.4 us
    gather x1, local copies, waits for them, and re-layouts, on_device(): suffix_rows = jnp.take(piece, gathered_index, axis=0, mode='clip')  3.96 us
  transfers between devices with their start and end apart: 1, of which 0 were waited for; matrix products, arithmetic and copies ran while one was open for 26% of the time, Pallas kernels for 0%

profile of v1, /device:TPU:0, one launch (start us, length us, event | category | flops | bytes accessed | tf_op | source)
XLA Modules:
  0.0 165.5 jit_solution(18030037125653893140)
XLA Ops:
  6.5 0.0 all-gather.2.cloned.1.call-start
  6.5 1.0 copy.25
  7.6 13.4 %all_to_all.19 = bf16[24,8,1024]{2,0,1:T(8,128)(2,1)} all-to-all(bf16[24,8,1024]{2,0,1:T(8,128)(2,1)S(1)} %bitcast.10), channel_id=1, replica_groups=mesh['row'=8,'col'=4] {'row'}, dimensions={1} | all-to-all | bytes 786432 | tf_op jit(solution)/shard_map/all_to_all | solution.py:311
  21.0 0.0 all-gather.2.cloned.1.call-update
  21.0 19.1 %copy.21.gate_ref = bf16[1024,7392]{1,0:T(8,128)(2,1)} copy(bf16[1024,7392]{0,1:T(8,128)(2,1)} %param.11) | data formatting | bytes 30277632 | tf_op args[4]
  40.1 0.0 slice-start
  40.1 0.0 slice-start.1
  40.1 0.0 copy-start
  40.1 0.0 copy-start.1
  40.1 0.0 copy-start.2
  40.1 19.1 %copy.22.up_ref = bf16[1024,7392]{1,0:T(8,128)(2,1)} copy(bf16[1024,7392]{0,1:T(8,128)(2,1)} %param.12) | data formatting | bytes 30277632 | tf_op args[5]
  59.1 1.1 slice.15
  60.2 0.0 slice-done
  60.2 1.1 pad.11.gate_tail
  61.4 1.1 pad.12.up_tail
  62.5 0.0 slice-done.1
  62.5 1.1 pad.13.down_tail
  63.6 0.0 copy-done
  63.6 0.0 copy-done.1
  63.6 0.2 select_reduce_fusion.1
  63.8 0.0 copy-done.2
  63.8 0.1 select_reduce_fusion
  63.9 0.0 all-gather.2.cloned.1.call-done
  64.0 4.0 %gather_fusion = bf16[256,1024]{1,0:T(8,128)(2,1)} fusion(bf16[768,1024]{1,0:T(8,128)(2,1)} %all-gather.2.cloned.1.call-done, s32[1024]{0:T(1024)S(1)} %pad_clamp_fusion), kind=kCustom, calls=%fused_computation | custom fusion | bytes 1049600 | tf_op jit(solution)/shard_map/jit(_take)/gather | solution.py:318
  67.9 89.1 %shard_map.73 = bf16[64,1024]{1,0:T(8,128)(2,1)} custom-call(bf16[256,1024]{1,0:T(8,128)(2,1)} %gather_fusion, bf16[1024,7392]{1,0:T(8,128)(2,1)} %copy.21.gate_ref, bf16[1024,7392]{1,0:T(8,128)(2,1)} %copy.22.up_ref, bf16[7392,1024]{1,0:T(8,128)(2,1)} %down_ref.1, bf16[1024,512]{1,0:T(8,128)(2,1)} %pad.11.gate_tail, bf16[1024,512]{1,0:T(8,128)(2,1)} %pad.12.up_tail, ...), custom_call_target="tpu_custom_call" | custom-call | flops 11626610688 | bytes 45416448 | tf_op jit(solution)/shard_map/pallas_call | solution.py:286
  157.1 1.6 copy.27
  (3 shorter events, 0.0 us)
Async XLA Ops:
  6.5 57.4 %all-gather.2.cloned.1.call-start = ((), (), s32[]{:S(2)}) async-start(), calls=%async_computation.1 | async-start | bytes 1966080 | tf_op jit(solution)/shard_map/all_gather | solution.py:317
  40.1 20.2 %slice-start = ((bf16[1024,7392]{1,0:T(8,128)(2,1)}), bf16[1024,224]{1,0:T(8,128)(2,1)S(1)}, s32[]{:S(2)}) async-start(bf16[1024,7392]{1,0:T(8,128)(2,1)} %copy.21.gate_ref), calls=%async_computation.2 | async-start | bytes 1048576 | tf_op jit(solution)/shard_map/slice | solution.py:249
  40.1 22.4 %slice-start.1 = ((bf16[7392,1024]{1,0:T(8,128)(2,1)}), bf16[224,1024]{1,0:T(8,128)(2,1)S(1)}, s32[]{:S(2)}) async-start(bf16[7392,1024]{1,0:T(8,128)(2,1)} %down_ref.1), calls=%async_computation.3 | async-start | bytes 917504 | tf_op jit(solution)/shard_map/slice | solution.py:251
  40.1 23.5 %copy-start = (s32[32]{0:T(128)S(1)}, s32[32]{0:T(128)}, u32[]{:S(2)}) copy-start(s32[32]{0:T(128)} %param.10) | copy-start | bytes 388
  40.1 23.5 %copy-start.1 = (s32[32]{0:T(128)S(1)}, s32[32]{0:T(128)}, u32[]{:S(2)}) copy-start(s32[32]{0:T(128)} %param.8) | copy-start | bytes 388
  40.1 23.7 %copy-start.2 = (s32[32]{0:T(128)S(1)}, s32[32]{0:T(128)}, u32[]{:S(2)}) copy-start(s32[32]{0:T(128)} %param.9) | copy-start | bytes 388
Sparse Core Ops, SparseCore 0:
  21.1 36.4 all-gather.1

commit v2 on v1

--- a/solution.py
+++ b/solution.py
@@ -8,9 +8,10 @@
 from jax.sharding import PartitionSpec as P
 
 TOK_DEV = 8
-CHUNK = 512
-LAG = 1
-WEIGHT_SLOTS = 4
+CHUNK = 256
+LAG = 2
+WEIGHT_SLOTS = 6
+PIECE = 128
 MESH = pl.DeviceIdType.MESH
 
 
@@ -31,11 +32,12 @@
 
 def layer_kernel(
     n, cols, chunks,
-    x_ref, gate_ref, up_ref, down_ref, gate_tail, up_tail, down_tail,
+    blocks_ref, place_ref, gate_ref, up_ref, down_ref,
     out_ref, *scratch,
 ):
     k = n.bit_length() - 1
-    tokens, width = x_ref.shape[0], gate_tail.shape[1]
+    tokens, width = place_ref.shape[0], CHUNK
+    rest = gate_ref.shape[0] - (chunks - 1) * width
     half = tokens // 2
     block = half >> k
     out_width = down_ref.shape[1]
@@ -45,7 +47,12 @@
     received = parts[8 : 8 + k]
     outgoing = [None] + parts[8 + k : 7 + 2 * k]
     kept = [None] + parts[7 + 2 * k : 6 + 3 * k]
-    send_sem, recv_sem, gather_send, gather_recv, weight_sem, col_send, col_recv = parts[6 + 3 * k :]
+    send_sem, recv_sem, gather_send, gather_recv, weight_sem, col_send, col_recv = parts[
+        6 + 3 * k : 13 + 3 * k
+    ]
+    x_ref, plane, own, line_out, line_in, block_send, block_recv, line_send, line_recv = parts[
+        13 + 3 * k :
+    ]
 
     me = lax.axis_index("row")
     my_col = lax.axis_index("col")
@@ -55,37 +62,51 @@
     places = [sum(bits[b] * (1 << (k - 1 - i)) for i, b in enumerate(order)) for order in orders]
 
     barrier = pltpu.get_barrier_semaphore()
-    for partner in partners:
-        pl.semaphore_signal(barrier, inc=1, device_id=(partner, my_col), device_id_type=MESH)
+    for step in range(1, n):
+        other = (me + step) % n
+        pl.semaphore_signal(barrier, inc=1, device_id=(other, my_col), device_id_type=MESH)
     for step in range(1, cols):
         other = (my_col + step) % cols
         pl.semaphore_signal(barrier, inc=1, device_id=(me, other), device_id_type=MESH)
-    pl.semaphore_wait(barrier, k + cols - 1)
-
-    def load(array, tail, buffer, kind, j, by_rows):
+    pl.semaphore_wait(barrier, n - 1 + cols - 1)
+
+    def weight_copy(kind, j, rows):
+        array, buffer = ((gate_ref, gate_w), (up_ref, up_w), (down_ref, down_w))[kind]
         slot = j % WEIGHT_SLOTS
-        sem = weight_sem.at[kind, slot]
-
+        return pltpu.make_async_copy(
+            array.at[pl.ds(pl.multiple_of(j * width, width), rows), :],
+            buffer.at[slot, pl.ds(0, rows), :],
+            weight_sem.at[kind, slot],
+        )
+
+    def load(kind, j):
         @pl.when(j < chunks - 1)
         def _():
-            at = pl.ds(pl.multiple_of(j * width, width), width)
-            piece = array.at[at, :] if by_rows else array.at[:, at]
-            pltpu.make_async_copy(piece, buffer.at[slot], sem).start()
+            weight_copy(kind, j, width).start()
 
         @pl.when(j == chunks - 1)
         def _():
-            pltpu.make_async_copy(tail, buffer.at[slot], sem).start()
-
-    def loaded(tail, buffer, kind, j):
-        slot = j % WEIGHT_SLOTS
-        pltpu.make_async_copy(tail, buffer.at[slot], weight_sem.at[kind, slot]).wait()
+            if rest < width:
+                buffer = (gate_w, up_w, down_w)[kind]
+                shape = (width - rest, buffer.shape[2])
+                buffer[j % WEIGHT_SLOTS, rest:, :] = jnp.zeros(shape, jnp.bfloat16)
+            weight_copy(kind, chunks - 1, rest).start()
+
+    def loaded(kind, j):
+        @pl.when(j < chunks - 1)
+        def _():
+            weight_copy(kind, j, width).wait()
+
+        @pl.when(j == chunks - 1)
+        def _():
+            weight_copy(kind, chunks - 1, rest).wait()
 
     def load_in(j):
-        load(gate_ref, gate_tail, gate_w, 0, j, False)
-        load(up_ref, up_tail, up_w, 1, j, False)
+        load(0, j)
+        load(1, j)
 
     def load_down(j):
-        load(down_ref, down_tail, down_w, 2, j, True)
+        load(2, j)
 
     def exchange(s, h, j):
         slot = j % slots
@@ -158,7 +179,7 @@
     def down(j):
         for h in range(2):
             gather(k - 1, h, j).wait_recv()
-        loaded(down_tail, down_w, 2, j)
+        loaded(2, j)
         total[...] += jnp.dot(
             hidden[j % hidden_slots], down_w[j % WEIGHT_SLOTS], preferred_element_type=jnp.float32
         )
@@ -168,17 +189,92 @@
 
     def project(j):
         slot = j % slots
-        loaded(gate_tail, gate_w, 0, j)
-        loaded(up_tail, up_w, 1, j)
+        loaded(0, j)
+        loaded(1, j)
         x = x_ref[...]
-        product[slot, :, :width] = jnp.dot(
-            x, gate_w[j % WEIGHT_SLOTS], preferred_element_type=jnp.float32
-        )
-        product[slot, :, width:] = jnp.dot(
-            x, up_w[j % WEIGHT_SLOTS], preferred_element_type=jnp.float32
+        features = (((1,), (1,)), ((), ()))
+        product[slot, :, :width] = lax.dot_general(
+            x, gate_w[j % WEIGHT_SLOTS], features, preferred_element_type=jnp.float32
+        )
+        product[slot, :, width:] = lax.dot_general(
+            x, up_w[j % WEIGHT_SLOTS], features, preferred_element_type=jnp.float32
         )
         for h in range(2):
             exchange(0, h, j).start()
+
+    pieces = own.shape[0]
+    deep = blocks_ref.shape[1]
+
+    def block_copy(step):
+        other = (me + step) % n
+        return pltpu.make_async_remote_copy(
+            src_ref=blocks_ref.at[other],
+            dst_ref=plane.at[pl.ds(pl.multiple_of(me * deep, deep), deep), :],
+            send_sem=block_send.at[step - 1],
+            recv_sem=block_recv.at[step - 1],
+            device_id=(other, my_col),
+            device_id_type=MESH,
+        )
+
+    def line_copy(way, f):
+        return pltpu.make_async_remote_copy(
+            src_ref=line_out.at[way, f],
+            dst_ref=line_in.at[way, f],
+            send_sem=line_send.at[way, f],
+            recv_sem=line_recv.at[way, f],
+            device_id=(me, (my_col + (1 if way == 0 else cols - 1)) % cols),
+            device_id_type=MESH,
+        )
+
+    def gather_rows():
+        copies = [block_copy(step) for step in range(1, n)]
+        for copy in copies:
+            copy.start()
+        plane[pl.ds(pl.multiple_of(me * deep, deep), deep), :] = blocks_ref[me]
+        column = lax.broadcasted_iota(jnp.int32, (tokens, n * deep), 1)
+        behind = [my_col, cols - 1 - my_col]
+        for way in range(2):
+            @pl.when(behind[way] == 0)
+            def _():
+                line_in[way] = jnp.zeros(line_in.shape[1:], jnp.bfloat16)
+
+        for copy in copies:
+            copy.wait()
+        for part in range(2):
+            pick = (column == place_ref[...] + part * (deep // 2)).astype(jnp.bfloat16)
+            rows = jnp.dot(pick, plane[...], preferred_element_type=jnp.float32)
+            rows = rows.astype(jnp.bfloat16)
+            for f in range(pieces // 2):
+                own[part * (pieces // 2) + f] = rows[:, f * PIECE : (f + 1) * PIECE]
+
+        def pass_on(u, carry):
+            for way in range(2):
+                f = u - 2 * behind[way]
+
+                @pl.when((f >= 0) & (f < pieces))
+                def _():
+                    @pl.when(behind[way] > 0)
+                    def _():
+                        line_copy(way, f).wait_recv()
+
+                    @pl.when(behind[way] < cols - 1)
+                    def _():
+                        line_out[way, f] = own[f] + line_in[way, f]
+                        line_copy(way, f).start()
+
+            return carry
+
+        lax.fori_loop(0, pieces + 2 * (cols - 1), pass_on, 0)
+        for f in range(pieces):
+            at = slice(f * PIECE, (f + 1) * PIECE)
+            x_ref[:, at] = own[f] + line_in[0, f] + line_in[1, f]
+
+    def end_gather():
+        for way in range(2):
+            @pl.when([my_col, cols - 1 - my_col][way] < cols - 1)
+            def _():
+                for f in range(pieces):
+                    line_copy(way, f).wait_send()
 
     steps = [project]
     steps += [functools.partial(halve, s) for s in range(1, k)]
@@ -191,6 +287,7 @@
         load_in(jnp.int32(j))
         load_down(jnp.int32(j))
     total[...] = jnp.zeros_like(total)
+    gather_rows()
     last = len(steps) - 1
 
     def round_of(t, carry):
@@ -215,6 +312,7 @@
 
     lax.fori_loop(0, chunks + last * LAG, round_of, 0)
 
+    end_gather()
     share = tokens // cols
     copies = []
     for step in range(1, cols):
@@ -238,17 +336,12 @@
     out_ref[...] = result.astype(jnp.bfloat16)
 
 
-def layer(x, gate_weight, up_weight, down_weight, n, cols):
-    tokens, depth = x.shape
-    units = gate_weight.shape[1]
+def layer(blocks, place, gate_weight, up_weight, down_weight, n, cols):
+    tokens = place.shape[0]
+    units, depth = gate_weight.shape
     out_width = down_weight.shape[1]
     width = CHUNK
     chunks = -(-units // width)
-    start = (chunks - 1) * width
-    short = width - (units - start)
-    gate_tail = jnp.pad(gate_weight[:, start:], ((0, 0), (0, short)))
-    up_tail = jnp.pad(up_weight[:, start:], ((0, 0), (0, short)))
-    down_tail = jnp.pad(down_weight[start:], ((0, short), (0, 0)))
     k = n.bit_length() - 1
     half = tokens // 2
     slots, hidden_slots = 2 * LAG, (k + 1) * LAG
@@ -259,8 +352,8 @@
         pltpu.VMEM((slots, tokens, 2 * width), f32),
         pltpu.VMEM((hidden_slots, tokens, width), bf16),
         pltpu.VMEM((tokens, out_width), f32),
-        pltpu.VMEM((WEIGHT_SLOTS, depth, width), bf16),
-        pltpu.VMEM((WEIGHT_SLOTS, depth, width), bf16),
+        pltpu.VMEM((WEIGHT_SLOTS, width, depth), bf16),
+        pltpu.VMEM((WEIGHT_SLOTS, width, depth), bf16),
         pltpu.VMEM((WEIGHT_SLOTS, width, out_width), bf16),
         pltpu.VMEM((cols - 1, share, out_width), bf16),
         pltpu.VMEM((cols - 1, share, out_width), bf16),
@@ -281,12 +374,24 @@
         dma((cols - 1,)),
         dma((cols - 1,)),
     ]
+    pieces = depth // PIECE
+    scratch += [
+        pltpu.VMEM((tokens, depth), bf16),
+        pltpu.VMEM((n * blocks.shape[1], depth // 2), bf16),
+        pltpu.VMEM((pieces, tokens, PIECE), bf16),
+        pltpu.VMEM((2, pieces, tokens, PIECE), bf16),
+        pltpu.VMEM((2, pieces, tokens, PIECE), bf16),
+        dma((n - 1,)),
+        dma((n - 1,)),
+        dma((2, pieces)),
+        dma((2, pieces)),
+    ]
     vmem = pl.BlockSpec(memory_space=pltpu.VMEM)
     hbm = pl.BlockSpec(memory_space=pl.ANY)
     return pl.pallas_call(
         functools.partial(layer_kernel, n, cols, chunks),
         out_shape=jax.ShapeDtypeStruct((share, out_width), bf16),
-        in_specs=[vmem] + [hbm] * 6,
+        in_specs=[vmem] * 2 + [hbm] * 3,
         out_specs=vmem,
         scratch_shapes=scratch,
         compiler_params=pltpu.CompilerParams(
@@ -297,7 +402,7 @@
             bytes_accessed=6 * depth * units,
             transcendentals=tokens * units // n,
         ),
-    )(x, gate_weight, up_weight, down_weight, gate_tail, up_tail, down_tail)
+    )(blocks, place, gate_weight, up_weight, down_weight)
 
 
 def on_device(
@@ -308,15 +413,18 @@
     slot_size = owned_rows.shape[0]
     total_rows = TOK_DEV * suffix_lengths.shape[0]
     source = source_rows(suffix_lengths, owner_map, prefix_lengths, total_rows, slot_size)
-    feature_rows = lax.all_to_all(owned_rows, "row", split_axis=1, concat_axis=0, tiled=True)
-    owner_index = source // slot_size
-    within = source % slot_size
-    gathered_index = (
-        owner_index % col_count * row_count + owner_index // col_count
-    ) * slot_size + within
-    piece = lax.all_gather(feature_rows, "col", axis=0, tiled=True)
-    suffix_rows = jnp.take(piece, gathered_index, axis=0, mode="clip")
-    return layer(suffix_rows, gate_weight, up_weight, down_weight, row_count, col_count)
+    owner = source // slot_size
+    deep = 2 * slot_size
+    place = jnp.where(
+        owner % col_count == lax.axis_index("col"),
+        owner // col_count * deep + source % slot_size,
+        -2 * deep,
+    )
+    blocks = owned_rows.reshape(slot_size, row_count, 2, -1).transpose(1, 2, 0, 3)
+    blocks = blocks.reshape(row_count, deep, -1)
+    return layer(
+        blocks, place[:, None], gate_weight.T, up_weight.T, down_weight, row_count, col_count
+    )
 
 
 def solution(mesh):

time: 167 us -> 115 us (0.69)
  local copies, waits for them, and re-layouts: 49.1 us -> 3.95 us
  Pallas kernels: 89.1 us -> 108 us
  between operations: 13.5 us -> 0.03 us
  blocking collectives: 13.4 us -> 0 us
  other arithmetic: 0.32 us -> 2.61 us
    unnamed x9 -> x1, local copies, waits for them, and re-layouts: 39.7 us -> 1.57 us
    pallas_call x1, Pallas kernels: 89.1 us -> 108 us  [layer(): pl.pallas_call(functools.partial(layer_kernel, n, cols, chunks), out_shap...]
    all_to_all x1 -> x0, blocking collectives: 13.4 us -> none  [on_device(): lax.all_to_all(owned_rows, 'row', split_axis=1, concat_axis=0, tiled=True)]
    gather x1 -> x0, local copies, waits for them, and re-layouts: 3.96 us -> none  [on_device(): suffix_rows = jnp.take(piece, gathered_index, axis=0, mode='clip')]
    pad x3 -> x0, local copies, waits for them, and re-layouts: 3.34 us -> none  [the longest x1 1.13 us: layer(): up_tail = jnp.pad(up_weight[:, start:], ((0, 0), (0, short)))]
    reshape x0 -> x2, local copies, waits for them, and re-layouts: none -> 2.24 us  [on_device(): owned_rows.reshape(slot_size, row_count, 2, -1).transpose(1, 2, 0, 3)]
  transfers between devices with their start and end apart: 1 -> 0, of which waited for: 0 -> 0; matrix products, arithmetic and copies ran while one was open for 26% -> 0% of each run, Pallas kernels for 0% -> 0%
where the time goes in v2:
time: 115 us
  Pallas kernels  108 us (94%)
  local copies, waits for them, and re-layouts  3.95 us (3%)
  other arithmetic  2.61 us (2%)
    pallas_call x1, Pallas kernels, layer(): pl.pallas_call(functools.partial(layer_kernel, n, cols, chunks), out_shap...  108 us

profile of v2, /device:TPU:0, one launch (start us, length us, event | category | flops | bytes accessed | tf_op | source)
XLA Modules:
  0.0 114.8 jit_solution(12895917206630239052)
XLA Ops:
  0.0 1.3 %reshape.135 = bf16[24,8,2,512]{3,2,1,0:T(2,128)(2,1)S(1)} reshape(bf16[24,8192]{1,0:T(8,128)(2,1)} %param.7) | data formatting | bytes 786432 | tf_op jit(solution)/shard_map/reshape | solution.py:423
  1.3 1.0 copy.11
  2.2 0.9 select_reduce_fusion.1
  3.2 0.7 fusion.10
  3.8 0.1 select_reduce_fusion
  3.9 0.1 copy.12
  4.1 0.9 fusion.3.place_ref
  5.0 108.2 %shard_map.73 = bf16[64,1024]{1,0:T(8,128)(2,1)} custom-call(bf16[8,48,512]{2,1,0:T(8,128)(2,1)} %bitcast.8, s32[256,1]{1,0:T(8,128)} %fusion.3.place_ref, bf16[7392,1024]{1,0:T(8,128)(2,1)} %bitcast.6, bf16[7392,1024]{1,0:T(8,128)(2,1)} %bitcast.7, bf16[7392,1024]{1,0:T(8,128)(2,1)} %down_ref.1), custom_call_target="tpu_custom_call" | custom-call | flops 11626610688 | bytes 45416448 | tf_op jit(solution)/shard_map/pallas_call | solution.py:391
  113.2 1.6 %copy.14 = bf16[64,1024]{1,0:T(8,128)(2,1)} copy(bf16[64,1024]{1,0:T(8,128)(2,1)} %shard_map.73) | data formatting | bytes 262144

commit v3 on v0

v3 whole, which is shorter than its diff:
```python
import functools

import jax
import jax.numpy as jnp
from jax import lax
from jax.experimental import pallas as pl
from jax.experimental.pallas import tpu as pltpu
from jax.sharding import PartitionSpec as P

TOK_DEV = 8
CHUNK = 512
BATCHES = 2
LAG = 2
WEIGHT_SLOTS = 4
PIECE = 128
MESH = pl.DeviceIdType.MESH


def layer_kernel(
    n, cols, chunks, batches,
    lengths_ref, owner_ref, prefix_ref, blocks_ref, gate_ref, up_ref, down_ref, out_ref,
    product, hidden, total, gate_w, up_w, down_w, col_out, col_in,
    x_ref, plane, own, line_out, line_in,
    send_sem, recv_sem, gather_send, gather_recv, weight_sem, col_send, col_recv,
    block_send, block_recv, line_send, line_recv, *stages,
):
    k = n.bit_length() - 1
    width, tokens = CHUNK, x_ref.shape[1]
    every = batches * chunks
    rest = gate_ref.shape[0] - (chunks - 1) * width
    block = tokens >> k
    part = tokens // cols
    slots, hidden_slots = 2 * LAG, (k + 1) * LAG
    received = stages[:k]
    outgoing = (None,) + stages[k : 2 * k - 1]
    kept = (None,) + stages[2 * k - 1 :]

    me = lax.axis_index("row")
    my_col = lax.axis_index("col")
    bits = [(me // (1 << b)) % 2 for b in range(k)]
    partners = [me + (1 - 2 * bits[b]) * (1 << b) for b in range(k)]
    orders = [list(range(k)), [0] + list(range(k - 1, 0, -1))]
    places = [sum(bits[b] * (1 << (k - 1 - i)) for i, b in enumerate(order)) for order in orders]

    def by_turn(values, j):
        return values[0] + (j % 2) * (values[1] - values[0])

    def bit_of(s, j):
        return by_turn([bits[order[s]] for order in orders], j)

    def partner_of(s, j):
        return by_turn([partners[order[s]] for order in orders], j)

    barrier = pltpu.get_barrier_semaphore()
    for step in range(1, n):
        other = (me + step) % n
        pl.semaphore_signal(barrier, inc=1, device_id=(other, my_col), device_id_type=MESH)
    for step in range(1, cols):
        other = (my_col + step) % cols
        pl.semaphore_signal(barrier, inc=1, device_id=(me, other), device_id_type=MESH)
    pl.semaphore_wait(barrier, n - 1 + cols - 1)

    def weight_copy(kind, j, rows):
        array, buffer = ((gate_ref, gate_w), (up_ref, up_w), (down_ref, down_w))[kind]
        slot = j % WEIGHT_SLOTS
        first = pl.multiple_of(j % chunks * width, width)
        return pltpu.make_async_copy(
            array.at[pl.ds(first, rows), :],
            buffer.at[slot, pl.ds(0, rows), :],
            weight_sem.at[kind, slot],
        )

    def load(kind, j):
        @pl.when(j % chunks < chunks - 1)
        def _():
            weight_copy(kind, j, width).start()

        @pl.when(j % chunks == chunks - 1)
        def _():
            if rest < width:
                buffer = (gate_w, up_w, down_w)[kind]
                shape = (width - rest, buffer.shape[2])
                buffer[j % WEIGHT_SLOTS, rest:, :] = jnp.zeros(shape, jnp.bfloat16)
            weight_copy(kind, j, rest).start()

    def loaded(kind, j):
        @pl.when(j % chunks < chunks - 1)
        def _():
            weight_copy(kind, j, width).wait()

        @pl.when(j % chunks == chunks - 1)
        def _():
            weight_copy(kind, j, rest).wait()

    def exchange(s, j):
        slot = j % slots
        size = tokens >> (s + 1)
        if s == 0:
            at = pl.multiple_of((1 - bits[0]) * size, size)
            source = product.at[slot, pl.ds(at, size), :]
        else:
            source = outgoing[s].at[slot]
        return pltpu.make_async_remote_copy(
            src_ref=source,
            dst_ref=received[s].at[slot],
            send_sem=send_sem.at[s, slot],
            recv_sem=recv_sem.at[s, slot],
            device_id=(partner_of(s, j), my_col),
            device_id_type=MESH,
        )

    def gather(i, j):
        slot = j % hidden_slots
        size = block << i
        at = pl.ds(pl.multiple_of(by_turn(places, j) // (1 << i) * size, size), size)
        return pltpu.make_async_remote_copy(
            src_ref=hidden.at[slot, at, :],
            dst_ref=hidden.at[slot, at, :],
            send_sem=gather_send.at[i, slot],
            recv_sem=gather_recv.at[i, slot],
            device_id=(partner_of(k - 1 - i, j), my_col),
            device_id_type=MESH,
        )

    def rows_of(s, j, first, size):
        slot = j % slots
        if s == 1:
            at = pl.multiple_of(bits[0] * (tokens >> 1) + first, size)
            mine = product[slot, pl.ds(at, size), :]
        else:
            mine = kept[s - 1][slot, pl.ds(first, size), :]
        return mine + received[s - 1][slot, pl.ds(first, size), :].astype(jnp.float32)

    def halve(s, j):
        size = tokens >> (s + 1)
        slot = j % slots
        bit = bit_of(s, j)
        away = pl.multiple_of((1 - bit) * size, size)
        stay = pl.multiple_of(bit * size, size)
        exchange(s - 1, j).wait()
        outgoing[s][slot] = rows_of(s, j, away, size).astype(jnp.bfloat16)
        exchange(s, j).start()
        kept[s][slot] = rows_of(s, j, stay, size)

    def activate(j):
        exchange(k - 1, j).wait()
        sums = rows_of(k, j, 0, block)
        gate, up = sums[:, :width], sums[:, width:]
        at = pl.multiple_of(by_turn(places, j) * block, block)
        value = (gate / (1.0 + jnp.exp(-gate)) * up).astype(jnp.bfloat16)
        hidden[j % hidden_slots, pl.ds(at, block), :] = value
        gather(0, j).start()

    def spread(i, j):
        gather(i - 1, j).wait_recv()
        gather(i, j).start()

    def down(j):
        gather(k - 1, j).wait_recv()
        loaded(2, j)
        total[j // chunks] += jnp.dot(
            hidden[j % hidden_slots], down_w[j % WEIGHT_SLOTS], preferred_element_type=jnp.float32
        )
        for i in range(k):
            gather(i, j).wait_send()

    def project(j):
        slot = j % slots
        loaded(0, j)
        loaded(1, j)
        x = x_ref[j // chunks]
        features = (((1,), (1,)), ((), ()))
        product[slot, :, :width] = lax.dot_general(
            x, gate_w[j % WEIGHT_SLOTS], features, preferred_element_type=jnp.float32
        )
        product[slot, :, width:] = lax.dot_general(
            x, up_w[j % WEIGHT_SLOTS], features, preferred_element_type=jnp.float32
        )
        exchange(0, j).start()

    steps = [project]
    steps += [functools.partial(halve, s) for s in range(1, k)]
    steps += [activate]
    steps += [functools.partial(spread, i) for i in range(1, k)]
    steps += [down]
    last = len(steps) - 1

    pieces = own.shape[1]
    deep = blocks_ref.shape[1]
    behind = [my_col, cols - 1 - my_col]
    line_steps = pieces + 2 * (cols - 1)

    def block_copy(step):
        other = (me + step) % n
        return pltpu.make_async_remote_copy(
            src_ref=blocks_ref.at[other],
            dst_ref=plane.at[pl.ds(pl.multiple_of(me * deep, deep), deep), :],
            send_sem=block_send.at[step - 1],
            recv_sem=block_recv.at[step - 1],
            device_id=(other, my_col),
            device_id_type=MESH,
        )

    def line_copy(batch, way, f):
        return pltpu.make_async_remote_copy(
            src_ref=line_out.at[batch, way, f],
            dst_ref=line_in.at[batch, way, f],
            send_sem=line_send.at[batch, way, f],
            recv_sem=line_recv.at[batch, way, f],
            device_id=(me, (my_col + (1 if way == 0 else cols - 1)) % cols),
            device_id_type=MESH,
        )

    def place_rows():
        count = lengths_ref.shape[1]
        f32 = jnp.float32
        lengths = lengths_ref[...].astype(f32)
        prefix = prefix_ref[...].astype(f32)
        owner = owner_ref[...]
        down_id = lax.broadcasted_iota(jnp.int32, (count, count), 0)
        over_id = lax.broadcasted_iota(jnp.int32, (count, count), 1)
        same = down_id == over_id
        lengths_down = jnp.sum(jnp.where(same, lengths, 0.0), axis=1, keepdims=True)
        prefix_down = jnp.sum(jnp.where(same, prefix, 0.0), axis=1, keepdims=True)
        before = (prefix_down > prefix) | ((prefix_down == prefix) & (down_id < over_id))
        starts = jnp.sum(jnp.where(before, lengths_down, 0.0), axis=0, keepdims=True)
        first = (owner // cols * deep).astype(f32) - starts
        first = jnp.where(owner % cols == my_col, first, -1e6)
        row = lax.broadcasted_iota(jnp.int32, (batches * tokens, 1), 0)
        batch, at = row // tokens, row % tokens
        token = ((at // part * batches + batch) * part + at % part).astype(f32)
        inside = (token >= starts) & (token < starts + lengths)
        return token + jnp.sum(jnp.where(inside, first, 0.0), axis=1, keepdims=True)

    def pick(batch, place):
        column = lax.broadcasted_iota(jnp.int32, (tokens, n * deep), 1).astype(jnp.float32)
        for side in range(2):
            chosen = (column == place + float(side * (deep // 2))).astype(jnp.bfloat16)
            rows = jnp.dot(chosen, plane[...], preferred_element_type=jnp.float32)
            rows = rows.astype(jnp.bfloat16)
            for f in range(pieces // 2):
                own[batch, side * (pieces // 2) + f] = rows[:, f * PIECE : (f + 1) * PIECE]

    def pass_on(batch, u):
        for way in range(2):
            f = u - 2 * behind[way]

            @pl.when((f >= 0) & (f < pieces))
            def _():
                @pl.when(behind[way] > 0)
                def _():
                    line_copy(batch, way, f).wait_recv()

                @pl.when(behind[way] < cols - 1)
                def _():
                    line_out[batch, way, f] = own[batch, f] + line_in[batch, way, f]
                    line_copy(batch, way, f).start()

    def join(batch):
        for f in range(pieces):
            at = slice(f * PIECE, (f + 1) * PIECE)
            x_ref[batch, :, at] = own[batch, f] + line_in[batch, 0, f] + line_in[batch, 1, f]

    def col_copy(batch, step):
        return pltpu.make_async_remote_copy(
            src_ref=col_out.at[batch, step - 1],
            dst_ref=col_in.at[batch, step - 1],
            send_sem=col_send.at[batch, step - 1],
            recv_sem=col_recv.at[batch, step - 1],
            device_id=(me, (my_col + step) % cols),
            device_id_type=MESH,
        )

    def send_cols(batch):
        for step in range(1, cols):
            other = (my_col + step) % cols
            rows = total[batch, pl.ds(pl.multiple_of(other * part, part), part), :]
            col_out[batch, step - 1] = rows.astype(jnp.bfloat16)
            col_copy(batch, step).start()

    for step in range(1, n):
        block_copy(step).start()
    ahead = WEIGHT_SLOTS - 1
    for j in range(min(ahead, every)):
        for kind in range(3):
            load(kind, jnp.int32(j))
    plane[pl.ds(pl.multiple_of(me * deep, deep), deep), :] = blocks_ref[me]
    total[...] = jnp.zeros_like(total)
    for way in range(2):
        @pl.when(behind[way] == 0)
        def _():
            for batch in range(batches):
                line_in[batch, way] = jnp.zeros(line_in.shape[2:], jnp.bfloat16)

    place = place_rows()
    for step in range(1, n):
        block_copy(step).wait()
    for batch in range(batches):
        pick(batch, place[batch * tokens : (batch + 1) * tokens])

    def first_line(u, carry):
        pass_on(0, u)
        return carry

    lax.fori_loop(0, line_steps, first_line, 0)
    join(0)
    per_round = -(-line_steps // chunks)

    def round_of(t, carry):
        @pl.when(t + ahead < every)
        def _():
            load(0, t + ahead)
            load(1, t + ahead)

        j_down = t - last * LAG + ahead

        @pl.when((j_down >= ahead) & (j_down < every))
        def _():
            load(2, j_down)

        for batch in range(1, batches):
            @pl.when(t == batch * chunks)
            def _():
                join(batch)

        for s in range(last, -1, -1):
            j = t - s * LAG

            @pl.when((j >= 0) & (j < every))
            def _():
                steps[s](j)

        for batch in range(1, batches):
            for q in range(per_round):
                pass_on(batch, (t - (batch - 1) * chunks) * per_round + q)

        for batch in range(batches):
            @pl.when(t == (batch + 1) * chunks - 1 + last * LAG)
            def _():
                send_cols(batch)

        return carry

    lax.fori_loop(0, every + last * LAG, round_of, 0)

    for batch in range(batches):
        for way in range(2):
            @pl.when(behind[way] < cols - 1)
            def _():
                for f in range(pieces):
                    line_copy(batch, way, f).wait_send()

    for batch in range(batches):
        result = total[batch, pl.ds(pl.multiple_of(my_col * part, part), part), :]
        for step in range(1, cols):
            col_copy(batch, step).wait()
            result = result + col_in[batch, step - 1].astype(jnp.float32)
        out_ref[batch * part : (batch + 1) * part, :] = result.astype(jnp.bfloat16)


def on_device(
    owned_rows, suffix_lengths, owner_map, prefix_lengths, gate_weight, up_weight, down_weight
):
    n, cols = lax.axis_size("row"), lax.axis_size("col")
    slot_size = owned_rows.shape[0]
    all_tokens = TOK_DEV * suffix_lengths.shape[0]
    depth, units = gate_weight.shape
    out_width = down_weight.shape[1]
    deep = 2 * slot_size
    blocks = owned_rows.reshape(slot_size, n, 2, depth // 2).transpose(1, 2, 0, 3)
    blocks = blocks.reshape(n, deep, depth // 2)

    width, batches = CHUNK, BATCHES
    tokens = all_tokens // batches
    chunks = -(-units // width)
    k = n.bit_length() - 1
    slots, hidden_slots = 2 * LAG, (k + 1) * LAG
    part = tokens // cols
    pieces = depth // PIECE
    bf16, f32 = jnp.bfloat16, jnp.float32
    dma = pltpu.SemaphoreType.DMA
    scratch = [
        pltpu.VMEM((slots, tokens, 2 * width), f32),
        pltpu.VMEM((hidden_slots, tokens, width), bf16),
        pltpu.VMEM((batches, tokens, out_width), f32),
        pltpu.VMEM((WEIGHT_SLOTS, width, depth), bf16),
        pltpu.VMEM((WEIGHT_SLOTS, width, depth), bf16),
        pltpu.VMEM((WEIGHT_SLOTS, width, out_width), bf16),
        pltpu.VMEM((batches, cols - 1, part, out_width), bf16),
        pltpu.VMEM((batches, cols - 1, part, out_width), bf16),
        pltpu.VMEM((batches, tokens, depth), bf16),
        pltpu.VMEM((n * deep, depth // 2), bf16),
        pltpu.VMEM((batches, pieces, tokens, PIECE), bf16),
        pltpu.VMEM((batches, 2, pieces, tokens, PIECE), bf16),
        pltpu.VMEM((batches, 2, pieces, tokens, PIECE), bf16),
        dma((k, slots)),
        dma((k, slots)),
        dma((k, hidden_slots)),
        dma((k, hidden_slots)),
        dma((3, WEIGHT_SLOTS)),
        dma((batches, cols - 1)),
        dma((batches, cols - 1)),
        dma((n - 1,)),
        dma((n - 1,)),
        dma((batches, 2, pieces)),
        dma((batches, 2, pieces)),
    ]
    sizes = [tokens >> (s + 1) for s in range(k)]
    scratch += [
        pltpu.VMEM((slots, size, 2 * width), f32 if s == 0 else bf16)
        for s, size in enumerate(sizes)
    ]
    scratch += [pltpu.VMEM((slots, size, 2 * width), bf16) for size in sizes[1:]]
    scratch += [pltpu.VMEM((slots, size, 2 * width), f32) for size in sizes[1:]]
    vmem = pl.BlockSpec(memory_space=pltpu.VMEM)
    hbm = pl.BlockSpec(memory_space=pl.ANY)
    return pl.pallas_call(
        functools.partial(layer_kernel, n, cols, chunks, batches),
        out_shape=jax.ShapeDtypeStruct((batches * part, out_width), bf16),
        in_specs=[vmem] * 4 + [hbm] * 3,
        out_specs=vmem,
        scratch_shapes=scratch,
        compiler_params=pltpu.CompilerParams(
            collective_id=0, has_side_effects=True, vmem_limit_bytes=56 * 1024 * 1024
        ),
        cost_estimate=pl.CostEstimate(
            flops=6 * all_tokens * depth * units,
            bytes_accessed=6 * depth * units * batches,
            transcendentals=all_tokens * units // n,
        ),
    )(
        suffix_lengths[None],
        owner_map[None],
        prefix_lengths[None],
        blocks,
        gate_weight.T,
        up_weight.T,
        down_weight,
    )


def solution(mesh):
    return jax.shard_map(
        on_device,
        mesh=mesh,
        in_specs=(
            P(("row", "col"), None),
            P(),
            P(),
            P(),
            P("row", "col"),
            P("row", "col"),
            P("col", "row"),
        ),
        out_specs=P("col", "row"),
        check_vma=False,
    )
```

time: 302 us -> 111 us (0.37)
  waiting for transfers between devices: 218 us -> 0 us
  Pallas kernels: 0 us -> 107 us
  matrix products: 46.6 us -> 0 us
  blocking collectives: 13.4 us -> 0 us
  between operations: 13.2 us -> 0.01 us
  other arithmetic: 5.89 us -> 0 us
    reduce_scatter x3 -> x0, waiting for transfers between devices: 149 us -> none  [the longest x1 72 us: on_device(): lax.psum_scatter(jnp.dot(block_rows, gate_weight, preferred_element_type=...]
    pallas_call x0 -> x1, Pallas kernels: none -> 107 us  [on_device(): pl.pallas_call(functools.partial(layer_kernel, n, cols, chunks, batches),...]
    all_gather x2 -> x0, waiting for transfers between devices: 69.8 us -> none  [the longest x1 35 us: on_device(): lax.all_gather(hidden_share, 'row', axis=0, tiled=True)]
    dot_general x3 -> x0, matrix products: 46.6 us -> none  [the longest x1 17.9 us: on_device(): jnp.dot(block_rows, gate_weight, preferred_element_type=jnp.float32)]
    all_to_all x1 -> x0, blocking collectives: 13.4 us -> none  [on_device(): lax.all_to_all(owned_rows, 'row', split_axis=1, concat_axis=0, tiled=True)]
    convert_element_type x2 -> x0, other arithmetic: 4.12 us -> none  [the longest x1 2.5 us: on_device(): hidden_share = (jax.nn.silu(gate_share) * up_share).astype(jnp.bfloat16)]
    gather x1 -> x0, local copies, waits for them, and re-layouts: 3.17 us -> none  [on_device(): jnp.take(piece, jnp.clip(gathered_index, 0, piece.shape[0] - 1), axis=0)]
  transfers between devices with their start and end apart: 5 -> 0, of which waited for: 5 -> 0; matrix products, arithmetic and copies ran while one was open for 7% -> 0% of each run, Pallas kernels for 0% -> 0%
where the time goes in v3:
time: 111 us
  Pallas kernels  107 us (96%)
  local copies, waits for them, and re-layouts  3.81 us (3%)
    pallas_call x1, Pallas kernels, on_device(): pl.pallas_call(functools.partial(layer_kernel, n, cols, chunks, batches),...  107 us
    reshape x2, local copies, waits for them, and re-layouts, on_device(): owned_rows.reshape(slot_size, n, 2, depth // 2).transpose(1, 2, 0, 3)  2.24 us

profile of v3, /device:TPU:0, one launch (start us, length us, event | category | flops | bytes accessed | tf_op | source)
XLA Modules:
  0.0 111.3 jit_solution(4311502168560262137)
XLA Ops:
  0.0 1.3 %reshape.6 = bf16[24,8,2,512]{3,2,1,0:T(2,128)(2,1)S(1)} reshape(bf16[24,8192]{1,0:T(8,128)(2,1)} %param.7) | data formatting | bytes 786432 | tf_op jit(solution)/shard_map/reshape | solution.py:370
  1.3 1.0 copy.8
  2.2 107.5 %shard_map.73 = bf16[64,1024]{1,0:T(8,128)(2,1)} custom-call(s32[1,32]{1,0:T(1,128)} %bitcast.11, s32[1,32]{1,0:T(1,128)} %bitcast.12, s32[1,32]{1,0:T(1,128)} %bitcast.13, bf16[8,48,512]{2,1,0:T(8,128)(2,1)} %bitcast.10, bf16[7392,1024]{1,0:T(8,128)(2,1)} %bitcast.8, bf16[7392,1024]{1,0:T(8,128)(2,1)} %bitcast.9, bf16[7392,1024]{1,0:T(8,128)(2,1)} %down_ref.1), custom_call_target="tpu_custom_call" | custom-call | flops 11626610688 | bytes 90832896 | tf_op jit(solution)/shard_map/pallas_call | solution.py:417
  109.7 1.6 %copy.10 = bf16[64,1024]{1,0:T(8,128)(2,1)} copy(bf16[64,1024]{1,0:T(8,128)(2,1)} %shard_map.73) | data formatting | bytes 262144

commit v4 on v3

--- a/solution.py
+++ b/solution.py
@@ -25,10 +25,10 @@
     block_send, block_recv, line_send, line_recv, *stages,
 ):
     k = n.bit_length() - 1
-    width, tokens = CHUNK, x_ref.shape[1]
+    width, tokens = CHUNK, x_ref.shape[2]
     every = batches * chunks
     rest = gate_ref.shape[0] - (chunks - 1) * width
-    block = tokens >> k
+    block = width >> k
     part = tokens // cols
     slots, hidden_slots = 2 * LAG, (k + 1) * LAG
     received = stages[:k]
@@ -94,10 +94,10 @@
 
     def exchange(s, j):
         slot = j % slots
-        size = tokens >> (s + 1)
+        size = width >> (s + 1)
         if s == 0:
             at = pl.multiple_of((1 - bits[0]) * size, size)
-            source = product.at[slot, pl.ds(at, size), :]
+            source = product.at[slot, :, pl.ds(at, size), :]
         else:
             source = outgoing[s].at[slot]
         return pltpu.make_async_remote_copy(
@@ -125,14 +125,14 @@
     def rows_of(s, j, first, size):
         slot = j % slots
         if s == 1:
-            at = pl.multiple_of(bits[0] * (tokens >> 1) + first, size)
-            mine = product[slot, pl.ds(at, size), :]
+            at = pl.multiple_of(bits[0] * (width >> 1) + first, size)
+            mine = product[slot, :, pl.ds(at, size), :]
         else:
-            mine = kept[s - 1][slot, pl.ds(first, size), :]
-        return mine + received[s - 1][slot, pl.ds(first, size), :].astype(jnp.float32)
+            mine = kept[s - 1][slot, :, pl.ds(first, size), :]
+        return mine + received[s - 1][slot, :, pl.ds(first, size), :].astype(jnp.float32)
 
     def halve(s, j):
-        size = tokens >> (s + 1)
+        size = width >> (s + 1)
         slot = j % slots
         bit = bit_of(s, j)
         away = pl.multiple_of((1 - bit) * size, size)
@@ -145,7 +145,7 @@
     def activate(j):
         exchange(k - 1, j).wait()
         sums = rows_of(k, j, 0, block)
-        gate, up = sums[:, :width], sums[:, width:]
+        gate, up = sums[0], sums[1]
         at = pl.multiple_of(by_turn(places, j) * block, block)
         value = (gate / (1.0 + jnp.exp(-gate)) * up).astype(jnp.bfloat16)
         hidden[j % hidden_slots, pl.ds(at, block), :] = value
@@ -158,8 +158,12 @@
     def down(j):
         gather(k - 1, j).wait_recv()
         loaded(2, j)
-        total[j // chunks] += jnp.dot(
-            hidden[j % hidden_slots], down_w[j % WEIGHT_SLOTS], preferred_element_type=jnp.float32
+        units = (((0,), (0,)), ((), ()))
+        total[j // chunks] += lax.dot_general(
+            hidden[j % hidden_slots],
+            down_w[j % WEIGHT_SLOTS],
+            units,
+            preferred_element_type=jnp.float32,
         )
         for i in range(k):
             gather(i, j).wait_send()
@@ -169,13 +173,10 @@
         loaded(0, j)
         loaded(1, j)
         x = x_ref[j // chunks]
-        features = (((1,), (1,)), ((), ()))
-        product[slot, :, :width] = lax.dot_general(
-            x, gate_w[j % WEIGHT_SLOTS], features, preferred_element_type=jnp.float32
-        )
-        product[slot, :, width:] = lax.dot_general(
-            x, up_w[j % WEIGHT_SLOTS], features, preferred_element_type=jnp.float32
-        )
+        product[slot, 0] = jnp.dot(
+            gate_w[j % WEIGHT_SLOTS], x, preferred_element_type=jnp.float32
+        )
+        product[slot, 1] = jnp.dot(up_w[j % WEIGHT_SLOTS], x, preferred_element_type=jnp.float32)
         exchange(0, j).start()
 
     steps = [project]
@@ -259,7 +260,8 @@
     def join(batch):
         for f in range(pieces):
             at = slice(f * PIECE, (f + 1) * PIECE)
-            x_ref[batch, :, at] = own[batch, f] + line_in[batch, 0, f] + line_in[batch, 1, f]
+            rows = own[batch, f] + line_in[batch, 0, f] + line_in[batch, 1, f]
+            x_ref[batch, at, :] = rows.T
 
     def col_copy(batch, step):
         return pltpu.make_async_remote_copy(
@@ -380,15 +382,15 @@
     bf16, f32 = jnp.bfloat16, jnp.float32
     dma = pltpu.SemaphoreType.DMA
     scratch = [
-        pltpu.VMEM((slots, tokens, 2 * width), f32),
-        pltpu.VMEM((hidden_slots, tokens, width), bf16),
+        pltpu.VMEM((slots, 2, width, tokens), f32),
+        pltpu.VMEM((hidden_slots, width, tokens), bf16),
         pltpu.VMEM((batches, tokens, out_width), f32),
         pltpu.VMEM((WEIGHT_SLOTS, width, depth), bf16),
         pltpu.VMEM((WEIGHT_SLOTS, width, depth), bf16),
         pltpu.VMEM((WEIGHT_SLOTS, width, out_width), bf16),
         pltpu.VMEM((batches, cols - 1, part, out_width), bf16),
         pltpu.VMEM((batches, cols - 1, part, out_width), bf16),
-        pltpu.VMEM((batches, tokens, depth), bf16),
+        pltpu.VMEM((batches, depth, tokens), bf16),
         pltpu.VMEM((n * deep, depth // 2), bf16),
         pltpu.VMEM((batches, pieces, tokens, PIECE), bf16),
         pltpu.VMEM((batches, 2, pieces, tokens, PIECE), bf16),
@@ -405,13 +407,13 @@
         dma((batches, 2, pieces)),
         dma((batches, 2, pieces)),
     ]
-    sizes = [tokens >> (s + 1) for s in range(k)]
+    sizes = [width >> (s + 1) for s in range(k)]
     scratch += [
-        pltpu.VMEM((slots, size, 2 * width), f32 if s == 0 else bf16)
+        pltpu.VMEM((slots, 2, size, tokens), f32 if s == 0 else bf16)
         for s, size in enumerate(sizes)
     ]
-    scratch += [pltpu.VMEM((slots, size, 2 * width), bf16) for size in sizes[1:]]
-    scratch += [pltpu.VMEM((slots, size, 2 * width), f32) for size in sizes[1:]]
+    scratch += [pltpu.VMEM((slots, 2, size, tokens), bf16) for size in sizes[1:]]
+    scratch += [pltpu.VMEM((slots, 2, size, tokens), f32) for size in sizes[1:]]
     vmem = pl.BlockSpec(memory_space=pltpu.VMEM)
     hbm = pl.BlockSpec(memory_space=pl.ANY)
     return pl.pallas_call(

time: 111 us -> 110 us (level)
  no operation moved by 1% of the time
where the time goes in v4:
time: 110 us
  Pallas kernels  106 us (96%)
  local copies, waits for them, and re-layouts  3.81 us (3%)
    pallas_call x1, Pallas kernels, on_device(): pl.pallas_call(functools.partial(layer_kernel, n, cols, chunks, batches),...  106 us
    reshape x2, local copies, waits for them, and re-layouts, on_device(): owned_rows.reshape(slot_size, n, 2, depth // 2).transpose(1, 2, 0, 3)  2.24 us

profile of v4, /device:TPU:0, one launch (start us, length us, event | category | flops | bytes accessed | tf_op | source)
XLA Modules:
  0.0 110.2 jit_solution(5801275126198010352)
XLA Ops:
  0.0 1.3 %reshape.6 = bf16[24,8,2,512]{3,2,1,0:T(2,128)(2,1)S(1)} reshape(bf16[24,8192]{1,0:T(8,128)(2,1)} %param.7) | data formatting | bytes 786432 | tf_op jit(solution)/shard_map/reshape | solution.py:372
  1.3 1.0 copy.8
  2.2 106.4 %shard_map.73 = bf16[64,1024]{1,0:T(8,128)(2,1)} custom-call(s32[1,32]{1,0:T(1,128)} %bitcast.11, s32[1,32]{1,0:T(1,128)} %bitcast.12, s32[1,32]{1,0:T(1,128)} %bitcast.13, bf16[8,48,512]{2,1,0:T(8,128)(2,1)} %bitcast.10, bf16[7392,1024]{1,0:T(8,128)(2,1)} %bitcast.8, bf16[7392,1024]{1,0:T(8,128)(2,1)} %bitcast.9, bf16[7392,1024]{1,0:T(8,128)(2,1)} %down_ref.1), custom_call_target="tpu_custom_call" | custom-call | flops 11626610688 | bytes 90832896 | tf_op jit(solution)/shard_map/pallas_call | solution.py:419
  108.6 1.6 %copy.10 = bf16[64,1024]{1,0:T(8,128)(2,1)} copy(bf16[64,1024]{1,0:T(8,128)(2,1)} %shard_map.73) | data formatting | bytes 262144

commit v5 on v4

--- a/solution.py
+++ b/solution.py
@@ -10,17 +10,16 @@
 TOK_DEV = 8
 CHUNK = 512
 BATCHES = 2
-LAG = 2
 WEIGHT_SLOTS = 4
 PIECE = 128
 MESH = pl.DeviceIdType.MESH
 
 
 def layer_kernel(
-    n, cols, chunks, batches,
-    lengths_ref, owner_ref, prefix_ref, blocks_ref, gate_ref, up_ref, down_ref, out_ref,
+    n, cols, chunks, batches, lag,
+    lengths_ref, owner_ref, prefix_ref, owned_ref, gate_ref, up_ref, down_ref, out_ref,
     product, hidden, total, gate_w, up_w, down_w, col_out, col_in,
-    x_ref, plane, own, line_out, line_in,
+    x_ref, blocks_ref, plane, own, line_out, line_in,
     send_sem, recv_sem, gather_send, gather_recv, weight_sem, col_send, col_recv,
     block_send, block_recv, line_send, line_recv, *stages,
 ):
@@ -30,7 +29,7 @@
     rest = gate_ref.shape[0] - (chunks - 1) * width
     block = width >> k
     part = tokens // cols
-    slots, hidden_slots = 2 * LAG, (k + 1) * LAG
+    slots, near_slots, hidden_slots = 2 * lag, lag + 1, (k + 1) * lag
     received = stages[:k]
     outgoing = (None,) + stages[k : 2 * k - 1]
     kept = (None,) + stages[2 * k - 1 :]
@@ -58,6 +57,14 @@
     for step in range(1, cols):
         other = (my_col + step) % cols
         pl.semaphore_signal(barrier, inc=1, device_id=(me, other), device_id_type=MESH)
+    side_width = blocks_ref.shape[2]
+    for r in range(n):
+        sides = [
+            owned_ref[:, (2 * r + side) * side_width : (2 * r + side + 1) * side_width]
+            for side in range(2)
+        ]
+        both = jnp.concatenate([side.astype(jnp.float32) for side in sides], axis=0)
+        blocks_ref[r] = both.astype(jnp.bfloat16)
     pl.semaphore_wait(barrier, n - 1 + cols - 1)
 
     def weight_copy(kind, j, rows):
@@ -97,9 +104,9 @@
         size = width >> (s + 1)
         if s == 0:
             at = pl.multiple_of((1 - bits[0]) * size, size)
-            source = product.at[slot, :, pl.ds(at, size), :]
+            source = product.at[j % near_slots, :, pl.ds(at, size), :]
         else:
-            source = outgoing[s].at[slot]
+            source = outgoing[s].at[j % near_slots]
         return pltpu.make_async_remote_copy(
             src_ref=source,
             dst_ref=received[s].at[slot],
@@ -126,14 +133,14 @@
         slot = j % slots
         if s == 1:
             at = pl.multiple_of(bits[0] * (width >> 1) + first, size)
-            mine = product[slot, :, pl.ds(at, size), :]
+            mine = product[j % near_slots, :, pl.ds(at, size), :]
         else:
-            mine = kept[s - 1][slot, :, pl.ds(first, size), :]
+            mine = kept[s - 1][j % near_slots, :, pl.ds(first, size), :]
         return mine + received[s - 1][slot, :, pl.ds(first, size), :].astype(jnp.float32)
 
     def halve(s, j):
         size = width >> (s + 1)
-        slot = j % slots
+        slot = j % near_slots
         bit = bit_of(s, j)
         away = pl.multiple_of((1 - bit) * size, size)
         stay = pl.multiple_of(bit * size, size)
@@ -169,7 +176,7 @@
             gather(i, j).wait_send()
 
     def project(j):
-        slot = j % slots
+        slot = j % near_slots
         loaded(0, j)
         loaded(1, j)
         x = x_ref[j // chunks]
@@ -314,7 +321,7 @@
             load(0, t + ahead)
             load(1, t + ahead)
 
-        j_down = t - last * LAG + ahead
+        j_down = t - last * lag + ahead
 
         @pl.when((j_down >= ahead) & (j_down < every))
         def _():
@@ -326,7 +333,7 @@
                 join(batch)
 
         for s in range(last, -1, -1):
-            j = t - s * LAG
+            j = t - s * lag
 
             @pl.when((j >= 0) & (j < every))
             def _():
@@ -337,13 +344,13 @@
                 pass_on(batch, (t - (batch - 1) * chunks) * per_round + q)
 
         for batch in range(batches):
-            @pl.when(t == (batch + 1) * chunks - 1 + last * LAG)
+            @pl.when(t == (batch + 1) * chunks - 1 + last * lag)
             def _():
                 send_cols(batch)
 
         return carry
 
-    lax.fori_loop(0, every + last * LAG, round_of, 0)
+    lax.fori_loop(0, every + last * lag, round_of, 0)
 
     for batch in range(batches):
         for way in range(2):
@@ -369,20 +376,19 @@
     depth, units = gate_weight.shape
     out_width = down_weight.shape[1]
     deep = 2 * slot_size
-    blocks = owned_rows.reshape(slot_size, n, 2, depth // 2).transpose(1, 2, 0, 3)
-    blocks = blocks.reshape(n, deep, depth // 2)
 
     width, batches = CHUNK, BATCHES
     tokens = all_tokens // batches
     chunks = -(-units // width)
     k = n.bit_length() - 1
-    slots, hidden_slots = 2 * LAG, (k + 1) * LAG
+    lag = 4 if tokens * width <= 1 << 16 else 2
+    slots, near_slots, hidden_slots = 2 * lag, lag + 1, (k + 1) * lag
     part = tokens // cols
     pieces = depth // PIECE
     bf16, f32 = jnp.bfloat16, jnp.float32
     dma = pltpu.SemaphoreType.DMA
     scratch = [
-        pltpu.VMEM((slots, 2, width, tokens), f32),
+        pltpu.VMEM((near_slots, 2, width, tokens), f32),
         pltpu.VMEM((hidden_slots, width, tokens), bf16),
         pltpu.VMEM((batches, tokens, out_width), f32),
         pltpu.VMEM((WEIGHT_SLOTS, width, depth), bf16),
@@ -391,6 +397,7 @@
         pltpu.VMEM((batches, cols - 1, part, out_width), bf16),
         pltpu.VMEM((batches, cols - 1, part, out_width), bf16),
         pltpu.VMEM((batches, depth, tokens), bf16),
+        pltpu.VMEM((n, deep, depth // 2), bf16),
         pltpu.VMEM((n * deep, depth // 2), bf16),
         pltpu.VMEM((batches, pieces, tokens, PIECE), bf16),
         pltpu.VMEM((batches, 2, pieces, tokens, PIECE), bf16),
@@ -412,12 +419,12 @@
         pltpu.VMEM((slots, 2, size, tokens), f32 if s == 0 else bf16)
         for s, size in enumerate(sizes)
     ]
-    scratch += [pltpu.VMEM((slots, 2, size, tokens), bf16) for size in sizes[1:]]
-    scratch += [pltpu.VMEM((slots, 2, size, tokens), f32) for size in sizes[1:]]
+    scratch += [pltpu.VMEM((near_slots, 2, size, tokens), bf16) for size in sizes[1:]]
+    scratch += [pltpu.VMEM((near_slots, 2, size, tokens), f32) for size in sizes[1:]]
     vmem = pl.BlockSpec(memory_space=pltpu.VMEM)
     hbm = pl.BlockSpec(memory_space=pl.ANY)
     return pl.pallas_call(
-        functools.partial(layer_kernel, n, cols, chunks, batches),
+        functools.partial(layer_kernel, n, cols, chunks, batches, lag),
         out_shape=jax.ShapeDtypeStruct((batches * part, out_width), bf16),
         in_specs=[vmem] * 4 + [hbm] * 3,
         out_specs=vmem,
@@ -434,7 +441,7 @@
         suffix_lengths[None],
         owner_map[None],
         prefix_lengths[None],
-        blocks,
+        owned_rows,
         gate_weight.T,
         up_weight.T,
         down_weight,

time: 110 us -> 106 us (0.964)
  local copies, waits for them, and re-layouts: 3.81 us -> 1.57 us
  Pallas kernels: 106 us -> 104 us
    pallas_call x1, Pallas kernels: 106 us -> 104 us  [on_device(): pl.pallas_call(functools.partial(layer_kernel, n, cols, chunks, batches,...]
    reshape x2 -> x0, local copies, waits for them, and re-layouts: 2.24 us -> none  [on_device(): owned_rows.reshape(slot_size, n, 2, depth // 2).transpose(1, 2, 0, 3)]
where the time goes in v5:
time: 106 us; the launch traced here: 105 us
  Pallas kernels  104 us (98%)
  local copies, waits for them, and re-layouts  1.57 us (1%)
    pallas_call x1, Pallas kernels, on_device(): pl.pallas_call(functools.partial(layer_kernel, n, cols, chunks, batches,...  104 us

profile of v5, /device:TPU:0, one launch (start us, length us, event | category | flops | bytes accessed | tf_op | source)
XLA Modules:
  0.0 105.4 jit_solution(18410717362494520964)
XLA Ops:
  0.0 103.9 %shard_map.73 = bf16[64,1024]{1,0:T(8,128)(2,1)} custom-call(s32[1,32]{1,0:T(1,128)} %bitcast.7, s32[1,32]{1,0:T(1,128)} %bitcast.8, s32[1,32]{1,0:T(1,128)} %bitcast.9, bf16[24,8192]{1,0:T(8,128)(2,1)} %owned_ref.1, bf16[7392,1024]{1,0:T(8,128)(2,1)} %bitcast.5, bf16[7392,1024]{1,0:T(8,128)(2,1)} %bitcast.6, bf16[7392,1024]{1,0:T(8,128)(2,1)} %down_ref.1), custom_call_target="tpu_custom_call" | custom-call | flops 11626610688 | bytes 90832896 | tf_op jit(solution)/shard_map/pallas_call | solution.py:426
  103.9 1.6 %copy.9 = bf16[64,1024]{1,0:T(8,128)(2,1)} copy(bf16[64,1024]{1,0:T(8,128)(2,1)} %shard_map.73) | data formatting | bytes 262144

commit v6 on v5

--- a/solution.py
+++ b/solution.py
@@ -196,7 +196,7 @@
     pieces = own.shape[1]
     deep = blocks_ref.shape[1]
     behind = [my_col, cols - 1 - my_col]
-    line_steps = pieces + 2 * (cols - 1)
+    hop, late_hop = 2, 6
 
     def block_copy(step):
         other = (me + step) % n
@@ -251,7 +251,7 @@
 
     def pass_on(batch, u):
         for way in range(2):
-            f = u - 2 * behind[way]
+            f = u - (hop if batch == 0 else late_hop) * behind[way]
 
             @pl.when((f >= 0) & (f < pieces))
             def _():
@@ -304,16 +304,15 @@
     place = place_rows()
     for step in range(1, n):
         block_copy(step).wait()
-    for batch in range(batches):
-        pick(batch, place[batch * tokens : (batch + 1) * tokens])
+    pick(0, place[:tokens])
 
     def first_line(u, carry):
         pass_on(0, u)
         return carry
 
-    lax.fori_loop(0, line_steps, first_line, 0)
+    lax.fori_loop(0, pieces + hop * (cols - 1), first_line, 0)
     join(0)
-    per_round = -(-line_steps // chunks)
+    per_round = -(-(pieces + late_hop * (cols - 1)) // chunks)
 
     def round_of(t, carry):
         @pl.when(t + ahead < every)
@@ -340,6 +339,10 @@
                 steps[s](j)
 
         for batch in range(1, batches):
+            @pl.when(t == (batch - 1) * chunks)
+            def _():
+                pick(batch, place[batch * tokens : (batch + 1) * tokens])
+
             for q in range(per_round):
                 pass_on(batch, (t - (batch - 1) * chunks) * per_round + q)
 

time: 106 us -> 103 us (0.972)
  Pallas kernels: 104 us -> 101 us
    pallas_call x1, Pallas kernels: 104 us -> 101 us  [on_device(): pl.pallas_call(functools.partial(layer_kernel, n, cols, chunks, batches,...]
where the time goes in v6:
time: 103 us; the launch traced here: 102 us
  Pallas kernels  101 us (98%)
  local copies, waits for them, and re-layouts  1.57 us (2%)
    pallas_call x1, Pallas kernels, on_device(): pl.pallas_call(functools.partial(layer_kernel, n, cols, chunks, batches,...  101 us

profile of v6, /device:TPU:0, one launch (start us, length us, event | category | flops | bytes accessed | tf_op | source)
XLA Modules:
  0.0 102.4 jit_solution(3382013819789905218)
XLA Ops:
  0.0 100.8 %shard_map.73 = bf16[64,1024]{1,0:T(8,128)(2,1)} custom-call(s32[1,32]{1,0:T(1,128)} %bitcast.7, s32[1,32]{1,0:T(1,128)} %bitcast.8, s32[1,32]{1,0:T(1,128)} %bitcast.9, bf16[24,8192]{1,0:T(8,128)(2,1)} %owned_ref.1, bf16[7392,1024]{1,0:T(8,128)(2,1)} %bitcast.5, bf16[7392,1024]{1,0:T(8,128)(2,1)} %bitcast.6, bf16[7392,1024]{1,0:T(8,128)(2,1)} %down_ref.1), custom_call_target="tpu_custom_call" | custom-call | flops 11626610688 | bytes 90832896 | tf_op jit(solution)/shard_map/pallas_call | solution.py:429
  100.8 1.6 %copy.9 = bf16[64,1024]{1,0:T(8,128)(2,1)} copy(bf16[64,1024]{1,0:T(8,128)(2,1)} %shard_map.73) | data formatting | bytes 262144
